TPU v7x, 32 devices: a whole 2x2x4 slice. The times are simulated.
32 devices in a mesh: replica: 1, shard: 8 (over z, x), tensor: 4 (over y, core).
Axes of the slice: x: 2, y: 2, z: 4, core: 2. Of those that a mesh axis runs over, the one named last changes fastest.
Arguments:
- inproj_grads: bfloat16 [1, 1536, 3328], P('replica', 'shard', 'tensor'), may hold values from -6 to 6
- inproj_error: float32 [1, 1536, 3328], P('replica', 'shard', 'tensor'), may hold values from -6 to 6
- inproj_weight: float32 [1536, 3328], P('shard', 'tensor'), may hold values from -6 to 6
- inproj_moment: float32 [1536, 3328], P('shard', 'tensor'), may hold values from -6 to 6
- inproj_query: float32 [3328, 32], P('tensor'), may hold values from -0.109375 to 0.109375
- outproj_grads: bfloat16 [1, 3072, 1536], P('replica', 'shard', 'tensor'), may hold values from -6 to 6
- outproj_error: float32 [1, 3072, 1536], P('replica', 'shard', 'tensor'), may hold values from -6 to 6
- outproj_weight: float32 [3072, 1536], P('shard', 'tensor'), may hold values from -6 to 6
- outproj_moment: float32 [3072, 1536], P('shard', 'tensor'), may hold values from -6 to 6
- outproj_query: float32 [1536, 32], P('tensor'), may hold values from -0.15625 to 0.15625
Outputs:
- inproj_master: float32 [1536, 3328], P('shard', 'tensor')
- inproj_velocity: float32 [1536, 3328], P('shard', 'tensor')
- inproj_residue: float32 [1, 1536, 3328], P('replica', 'shard', 'tensor')
- inproj_basis: float32 [3328, 32], P('tensor')
- outproj_master: float32 [3072, 1536], P('shard', 'tensor')
- outproj_velocity: float32 [3072, 1536], P('shard', 'tensor')
- outproj_residue: float32 [1, 3072, 1536], P('replica', 'shard', 'tensor')
- outproj_basis: float32 [1536, 32], P('tensor')
All inputs are finite; a program needn't handle non-finite values.
Results may differ from a plain program's by a relative error of at most 0.0003.
Values sent between devices are 32-bit elements; how exact they have to be, the bound alone decides.
A program may use at most 64 MiB of HBM per device.

v0:
```python
import jax
import jax.numpy as jnp
from jax import lax
from jax.sharding import PartitionSpec as P

ROUNDS = 2
NS_STEPS = 4


MOMENTUM_DECAY = 0.9
LEARN_RATE = 0.1
EPSILON = 1e-06


def precise_dot(left, right):
    return jnp.dot(left, right, precision=lax.Precision.HIGHEST, preferred_element_type=jnp.float32)


def inverse_root(gram_sum):
    identity = jnp.eye(gram_sum.shape[0], dtype=jnp.float32)
    norm_scale = jnp.sqrt(jnp.sum(gram_sum * gram_sum) + EPSILON)
    current = gram_sum / norm_scale
    inverse = identity
    for sweep in range(NS_STEPS):
        middle = 0.5 * (3.0 * identity - precise_dot(inverse, current))
        current = precise_dot(current, middle)
        inverse = precise_dot(middle, inverse)
    return inverse / jnp.sqrt(norm_scale)


def finish(merged, orthonormal, query, weight, moment):
    approx = precise_dot(orthonormal, query.T)
    residue = (merged - approx)[None]
    velocity = MOMENTUM_DECAY * moment + approx
    master = weight - LEARN_RATE * velocity
    return (master, velocity, residue, query)


def per_device(
    inproj_grads,
    inproj_error,
    inproj_weight,
    inproj_moment,
    inproj_query,
    outproj_grads,
    outproj_error,
    outproj_weight,
    outproj_moment,
    outproj_query,
):
    replicas = lax.axis_size("replica")
    merged_in = inproj_grads[0].astype(jnp.float32) + inproj_error[0]
    merged_out = outproj_grads[0].astype(jnp.float32) + outproj_error[0]
    query_in = inproj_query
    query_out = outproj_query
    for power_round in range(ROUNDS):
        partial_in = precise_dot(merged_in, query_in)
        partial_out = precise_dot(merged_out, query_out)
        summed_in, summed_out = lax.psum((partial_in, partial_out), ("replica", "tensor"))
        projected_in = summed_in / replicas
        projected_out = summed_out / replicas
        gram_in, gram_out = lax.psum(
            (
                precise_dot(projected_in.T, projected_in),
                precise_dot(projected_out.T, projected_out),
            ),
            "shard",
        )
        ortho_in = precise_dot(projected_in, inverse_root(gram_in))
        ortho_out = precise_dot(projected_out, inverse_root(gram_out))
        column_in = jnp.einsum(
            "nm,nk->mk",
            merged_in,
            ortho_in,
            precision=lax.Precision.HIGHEST,
            preferred_element_type=jnp.float32,
        )
        column_out = jnp.einsum(
            "nm,nk->mk",
            merged_out,
            ortho_out,
            precision=lax.Precision.HIGHEST,
            preferred_element_type=jnp.float32,
        )
        summed_cin, summed_cout = lax.psum((column_in, column_out), ("replica", "shard"))
        query_in = summed_cin / replicas
        query_out = summed_cout / replicas
    first = finish(merged_in, ortho_in, query_in, inproj_weight, inproj_moment)
    second = finish(merged_out, ortho_out, query_out, outproj_weight, outproj_moment)
    return (first[0], first[1], first[2], first[3], second[0], second[1], second[2], second[3])


def solution(mesh):
    return jax.shard_map(
        per_device,
        mesh=mesh,
        in_specs=(
            P("replica", "shard", "tensor"),
            P("replica", "shard", "tensor"),
            P("shard", "tensor"),
            P("shard", "tensor"),
            P("tensor", None),
            P("replica", "shard", "tensor"),
            P("replica", "shard", "tensor"),
            P("shard", "tensor"),
            P("shard", "tensor"),
            P("tensor", None),
        ),
        out_specs=(
            P("shard", "tensor"),
            P("shard", "tensor"),
            P("replica", "shard", "tensor"),
            P("tensor", None),
            P("shard", "tensor"),
            P("shard", "tensor"),
            P("replica", "shard", "tensor"),
            P("tensor", None),
        ),
        check_vma=False,
    )
```

profile of v0, /device:TPU:0, one launch (start us, length us, event | category | flops | bytes accessed | tf_op | source)
XLA Modules:
  0.0 377.3 jit_solution(3860488859477507557)
XLA Ops:
  7.2 1.9 fusion.31
  9.1 13.4 %psum.90 = f32[384,32]{0,1:T(8,128)S(1)} all-reduce(f32[384,32]{0,1:T(8,128)S(1)} %fusion.31), channel_id=1, replica_groups=mesh['replica'=1,'shard'=8,'tensor'=4] {'replica','tensor'}, use_global_device_ids=true, to_apply=%region_8.0 | all-reduce | flops 12288 | bytes 98304 | tf_op jit(solution)/shard_map/psum | solution.py:59
  22.7 37.4 %psum.91 = f32[32,32]{1,0:T(8,128)S(1)} all-reduce(f32[32,32]{1,0:T(8,128)S(1)} %fusion.54), channel_id=1, replica_groups=mesh['replica'=1,'shard'=8,'tensor'=4] {'shard'}, use_global_device_ids=true, to_apply=%region_9.0 | all-reduce | flops 1024 | bytes 8192 | tf_op jit(solution)/shard_map/psum | solution.py:62
  60.1 0.6 multiply_reduce_fusion.1
  63.6 1.1 fusion.29
  64.7 35.2 %psum.92 = f32[384,32]{1,0:T(8,128)S(1)} all-reduce(f32[384,32]{1,0:T(8,128)S(1)} %fusion.29), channel_id=1, replica_groups=mesh['replica'=1,'shard'=8,'tensor'=4] {'replica','shard'}, use_global_device_ids=true, to_apply=%region_11.0 | all-reduce | flops 12288 | bytes 98304 | tf_op jit(solution)/shard_map/psum | solution.py:85
  99.9 1.3 fusion.27
  101.3 1.4 fusion.22
  102.8 27.9 %all-reduce.11.cloned.1.call-done = (f32[192,32]{0,1:T(8,128)}, f32[384,32]{0,1:T(8,128)}) async-done(((f32[192,32]{0,1:T(8,128)}, f32[384,32]{0,1:T(8,128)}), (f32[192,32]{0,1:T(8,128)}, f32[384,32]{0,1:T(8,128)})) %all-reduce.11.cloned.1.call-update) | async-done | bytes 73744 | tf_op jit(solution)/shard_map/psum | solution.py:59
  130.7 1.0 fusion.42
  131.9 37.2 %all-reduce.1 = (f32[32,32]{1,0:T(8,128)S(1)}, f32[32,32]{1,0:T(8,128)S(1)}) all-reduce(f32[32,32]{1,0:T(8,128)S(1)} %fusion.42, f32[32,32]{1,0:T(8,128)S(1)} %fusion.60), channel_id=1, replica_groups=mesh['replica'=1,'shard'=8,'tensor'=4] {'shard'}, use_global_device_ids=true, to_apply=%region_1.0 | all-reduce | flops 2048 | bytes 16384 | tf_op jit(solution)/shard_map/psum | solution.py:62
  169.1 0.6 multiply_reduce_fusion
  174.7 0.6 copy-done.9
  175.7 2.3 fusion.20
  178.6 69.1 %all-reduce.7.cloned.1.call-done = f32[832,32]{1,0:T(8,128)} async-done(((f32[832,32]{1,0:T(8,128)}), f32[832,32]{1,0:T(8,128)}) %all-reduce.7.cloned.1.call-update) | async-done | bytes 106512 | tf_op jit(solution)/shard_map/psum | solution.py:85
  247.7 1.8 fusion.18
  249.6 10.3 %psum.87 = f32[192,32]{0,1:T(8,128)S(1)} all-reduce(f32[192,32]{0,1:T(8,128)S(1)} %fusion.18), channel_id=1, replica_groups=mesh['replica'=1,'shard'=8,'tensor'=4] {'replica','tensor'}, use_global_device_ids=true, to_apply=%region_4.0 | all-reduce | flops 6144 | bytes 49152 | tf_op jit(solution)/shard_map/psum | solution.py:59
  260.0 36.0 %all-reduce = (f32[32,32]{1,0:T(8,128)S(1)}, f32[384,32]{0,1:T(8,128)S(1)}) all-reduce(f32[32,32]{1,0:T(8,128)S(1)} %fusion.48, f32[384,32]{0,1:T(8,128)S(1)} %fusion.25), channel_id=1, replica_groups=mesh['replica'=1,'shard'=8,'tensor'=4] {'shard'}, use_global_device_ids=true, to_apply=%region_5.0 | all-reduce | flops 13312 | bytes 106496 | tf_op jit(solution)/shard_map/psum | solution.py:62
  296.0 0.6 multiply_reduce_fusion.2
  299.2 1.2 fusion.16
  300.5 3.3 multiply_subtract_fusion.1
  303.8 63.2 %all-reduce.9.cloned.1.call-done = f32[832,32]{0,1:T(8,128)} async-done(((f32[832,32]{0,1:T(8,128)}), f32[832,32]{0,1:T(8,128)}) %all-reduce.9.cloned.1.call-update) | async-done | bytes 106512 | tf_op jit(solution)/shard_map/psum | solution.py:85
  367.0 3.1 multiply_subtract_fusion
  370.1 0.6 copy.22
  (79 shorter events, 9.0 us)
Async XLA Ops:
  7.2 94.1 %copy-start = (f32[832,32]{0,1:T(8,128)S(1)}, f32[832,32]{0,1:T(8,128)}, u32[]{:S(2)}) copy-start(f32[832,32]{0,1:T(8,128)} %param.14) | copy-start | bytes 319492
  7.2 123.5 %all-reduce.11.cloned.1.call-start = ((), (), s32[]{:S(2)}) async-start(), calls=%async_computation.2 | async-start | bytes 163840 | tf_op jit(solution)/shard_map/psum | solution.py:59
  9.1 54.5 %copy-start.2 = (f32[1,384,384]{2,1,0:T(8,128)S(1)}, f32[1,384,384]{2,1,0:T(8,128)}, u32[]{:S(2)}) copy-start(f32[1,384,384]{2,1,0:T(8,128)} %param.16) | copy-start | bytes 1769476
  62.0 1.6 copy-start.4
  64.7 36.5 %copy-start.1 = (f32[1,192,832]{2,1,0:T(8,128)S(1)}, f32[1,192,832]{2,1,0:T(8,128)}, u32[]{:S(2)}) copy-start(f32[1,192,832]{2,1,0:T(8,128)} %param.11) | copy-start | bytes 1916932
  99.9 1.4 copy-start.3
  102.7 145.0 %all-reduce.7.cloned.1.call-start = ((), (), s32[]{:S(2)}) async-start(), calls=%async_computation | async-start | bytes 851968 | tf_op jit(solution)/shard_map/psum | solution.py:85
  130.7 1.0 copy-start.8
  174.6 0.8 copy-start.9
  178.1 189.0 %all-reduce.9.cloned.1.call-start = ((), (), s32[]{:S(2)}) async-start(), calls=%async_computation.1 | async-start | bytes 229376 | tf_op jit(solution)/shard_map/psum | solution.py:85
  296.0 4.5 %copy-start.10 = (f32[384,32]{0,1:T(8,128)}, f32[384,32]{0,1:T(8,128)S(1)}, u32[]{:S(2)}) copy-start(f32[384,32]{0,1:T(8,128)S(1)} %get-tuple-element.29) | copy-start | bytes 147460
  300.5 66.6 %copy-start.5 = (f32[192,832]{1,0:T(8,128)S(1)}, f32[192,832]{1,0:T(8,128)}, u32[]{:S(2)}) copy-start(f32[192,832]{1,0:T(8,128)} %param.12) | copy-start | bytes 1916932
  300.5 66.6 %copy-start.6 = (f32[192,832]{1,0:T(8,128)S(1)}, f32[192,832]{1,0:T(8,128)}, u32[]{:S(2)}) copy-start(f32[192,832]{1,0:T(8,128)} %param.13) | copy-start | bytes 1916932
  367.0 3.1 copy-start.7
Sparse Core Ops, SparseCore 0:
  102.8 27.8 all-reduce.10
  178.2 69.4 all-reduce.6
  300.6 66.4 all-reduce.8
where the time goes:
time: 378 us; the launch traced here: 377 us
  blocking collectives  169 us (45%)
  waiting for transfers between devices  160 us (42%)
  matrix products  27.3 us (7%)
  between operations  17.1 us (5%)
    psum x2, waiting for transfers between devices, per_device(): lax.psum((column_in, column_out), ('replica', 'shard'))  132 us
    psum x3, blocking collectives, per_device(): lax.psum((precise_dot(projected_in.T, projected_in), precise_dot(projecte...  111 us
    psum x1, blocking collectives, per_device(): lax.psum((column_in, column_out), ('replica', 'shard'))  35.2 us
    psum x1, waiting for transfers between devices, per_device(): lax.psum((partial_in, partial_out), ('replica', 'tensor'))  27.9 us
    psum x2, blocking collectives, per_device(): lax.psum((partial_in, partial_out), ('replica', 'tensor'))  23.6 us
    dot_general x58, matrix products, precise_dot(): jnp.dot(left, right, precision=lax.Precision.HIGHEST, preferred_element_t...  22.1 us
  transfers between devices with their start and end apart: 3, of which 3 were waited for; matrix products, arithmetic and copies ran while one was open for 1% of the time, Pallas kernels for 0%

commit v1 on v0

v1 whole, which is shorter than its diff:
```python
import functools
import math

import jax
import jax.numpy as jnp
from jax import lax
from jax.experimental import pallas as pl
from jax.experimental.pallas import tpu as pltpu
from jax.sharding import PartitionSpec as P

ROUNDS = 2
NS_STEPS = 4
MOMENTUM_DECAY = 0.9
LEARN_RATE = 0.1
EPSILON = 1e-06
LANES = 128
MESH = pl.DeviceIdType.MESH
F32 = jnp.float32
BF16 = jnp.bfloat16


def up(value, multiple):
    return -(-value // multiple) * multiple


def split(value):
    high = value.astype(BF16)
    low = (value - high.astype(F32)).astype(BF16)
    return high, low


def dot(left, right, contract):
    return lax.dot_general(left, right, ((contract[:1], contract[1:]), ((), ())), preferred_element_type=F32)


def exact(left, right, contract=(1, 0)):
    return lax.dot_general(
        left,
        right,
        ((contract[:1], contract[1:]), ((), ())),
        precision=lax.Precision.HIGHEST,
        preferred_element_type=F32,
    )


def by_matrix(factor, high_ref, low_ref, contract):
    rank = factor.shape[0]
    high, low = split(factor)
    both = dot(jnp.concatenate([high, low], axis=0), high_ref[...], contract)
    return both[:rank] + both[rank:] + dot(high, low_ref[...], contract)


def inverse_roots(grams):
    rank = grams[0].shape[0]
    identity = (
        lax.broadcasted_iota(jnp.int32, (rank, rank), 0) == lax.broadcasted_iota(jnp.int32, (rank, rank), 1)
    ).astype(F32)
    scales = [jnp.sqrt(jnp.sum(gram * gram, keepdims=True) + EPSILON) for gram in grams]
    currents = [gram / scale for gram, scale in zip(grams, scales)]
    inverses = [identity for gram in grams]
    for sweep in range(NS_STEPS):
        products = [current if sweep == 0 else exact(inverse, current) for inverse, current in zip(inverses, currents)]
        middles = [0.5 * (3.0 * identity - product) for product in products]
        inverses = [middle if sweep == 0 else exact(middle, inverse) for middle, inverse in zip(middles, inverses)]
        if sweep < NS_STEPS - 1:
            currents = [exact(current, middle) for current, middle in zip(currents, middles)]
    return [inverse / jnp.sqrt(scale) for inverse, scale in zip(inverses, scales)]


class Group:
    def __init__(self, axes, sizes, rank, width):
        self.axes = axes
        self.sizes = sizes
        self.count = math.prod(sizes)
        down = math.gcd(self.count, max(rank // 8, 1))
        self.across = self.count // down
        self.rows = rank // down
        self.total = up(width, LANES * self.across)
        self.width = self.total // self.across

    def me(self):
        index = 0
        for axis, size in zip(self.axes, self.sizes):
            index = index * size + lax.axis_index(axis)
        return index

    def device(self, index):
        place = {name: lax.axis_index(name) for name in ("replica", "shard", "tensor")}
        for axis, size in reversed(list(zip(self.axes, self.sizes))):
            place[axis] = lax.rem(index, size)
            index = lax.div(index, size)
        return (place["replica"], place["shard"], place["tensor"])

    def peers(self):
        me = self.me()
        return [lax.rem(me + step, self.count) for step in range(1, self.count)]

    def piece(self, index):
        if self.across == 1:
            row, lane = index * self.rows, 0
        else:
            row = lax.div(index, self.across) * self.rows
            lane = pl.multiple_of(lax.rem(index, self.across) * self.width, LANES)
        return (pl.ds(pl.multiple_of(row, 8), self.rows), pl.ds(lane, self.width))

    def slots(self):
        return max(self.count - 1, 1)


def send(group, source, target, sends, receives):
    copies = []
    for step, peer in enumerate(group.peers()):
        copy = pltpu.make_async_remote_copy(
            src_ref=source(peer),
            dst_ref=target(step),
            send_sem=sends.at[step],
            recv_sem=receives.at[step],
            device_id=group.device(peer),
            device_id_type=MESH,
        )
        copy.start()
        copies.append(copy)
    return copies


def factors_kernel(
    left,
    right,
    gram,
    replicas,
    grads_in,
    error_in,
    query_in,
    grads_out,
    error_out,
    query_out,
    ortho_ref,
    stack_ref,
    basis_in,
    basis_out,
    in_high,
    in_low,
    out_high,
    out_low,
    left_part,
    left_slots,
    left_sum,
    right_part,
    right_slots,
    right_sum,
    gram_part,
    gram_slots,
    left_sems,
    right_sems,
    gram_sems,
):
    rank = query_in.shape[0]
    half = rank // 2
    rows_in, cols_in = in_high.shape
    rows_out, cols_out = out_high.shape
    row_at, col_at = up(rows_out, LANES), up(cols_out, LANES)
    barrier = pltpu.get_barrier_semaphore()
    greeted = 0
    for group in (left, right, gram):
        for peer in group.peers():
            pl.semaphore_signal(barrier, inc=1, device_id=group.device(peer), device_id_type=MESH)
            greeted += 1

    merged = grads_in[0].astype(F32) + error_in[0]
    in_high[...], in_low[...] = split(merged)
    merged = grads_out[0].astype(F32) + error_out[0]
    out_high[...], out_low[...] = split(merged)
    left_part[...] = jnp.zeros_like(left_part)
    right_part[...] = jnp.zeros_like(right_part)

    def reduce(group, turn, part, slots, total, sems):
        me = group.me()
        copies = send(group, lambda peer: part.at[turn].at[group.piece(peer)], lambda step: slots.at[turn, step], sems.at[turn, 0], sems.at[turn, 1])
        for copy in copies:
            copy.wait_recv()
        mine = part.at[turn].at[group.piece(me)][...]
        for step in range(group.count - 1):
            mine = mine + slots[turn, step]
        if replicas > 1:
            mine = mine * (1.0 / replicas)
        own = total.at[turn].at[group.piece(me)]
        own[...] = mine
        again = send(group, lambda peer: own, lambda step: own, sems.at[turn, 2], sems.at[turn, 3])
        return copies + again, again

    pending = []
    inverses = None
    for turn in range(ROUNDS):
        if turn == 0:
            factor_in, factor_out = query_in[...], query_out[...]
        left_part[turn, :, :rows_out] = by_matrix(factor_out, out_high, out_low, (1, 1))
        left_part[turn, :, row_at : row_at + rows_in] = by_matrix(factor_in, in_high, in_low, (1, 1))
        if turn == 0:
            pl.semaphore_wait(barrier, greeted)
        copies, gathers = reduce(left, turn, left_part, left_slots, left_sum, left_sems)
        pending += copies
        if turn > 0:
            inverses = gram_roots(gram, turn - 1, gram_part, gram_slots, gram_copies, half)
        for copy in gathers:
            copy.wait_recv()
        projected = left_sum[turn]
        projected_out = projected[:, :rows_out]
        projected_in = projected[:, row_at : row_at + rows_in]
        if turn > 0:
            projected_in = exact(inverses[0], projected_in)
            projected_out = exact(inverses[1], projected_out)
        place = 0
        for value in (projected_in, projected_out):
            product = exact(value, value, (1, 1))
            for start in (0, half):
                gram_part[turn, :, place : place + rank] = product[start : start + half]
                place += rank
        gram_copies = send(
            gram,
            lambda peer: gram_part.at[turn],
            lambda step: gram_slots.at[turn, step],
            gram_sems.at[turn, 0],
            gram_sems.at[turn, 1],
        )
        pending += gram_copies
        right_part[turn, :, :cols_out] = by_matrix(projected_out, out_high, out_low, (1, 0))
        right_part[turn, :, col_at : col_at + cols_in] = by_matrix(projected_in, in_high, in_low, (1, 0))
        copies, gathers = reduce(right, turn, right_part, right_slots, right_sum, right_sems)
        pending += copies
        if turn == ROUNDS - 1:
            inverses = gram_roots(gram, turn, gram_part, gram_slots, gram_copies, half)
            for value, inverse, start, size in (
                (projected_out, inverses[1], 0, rows_out),
                (projected_in, inverses[0], row_at, rows_in),
            ):
                high, low = split(exact(inverse, value))
                tall = jnp.concatenate([high, high, low], axis=0).astype(F32)
                ortho_ref[start : start + size, :] = jnp.transpose(tall).astype(BF16)
        for copy in gathers:
            copy.wait_recv()
        factor_out = right_sum[turn, :, :cols_out]
        factor_in = right_sum[turn, :, col_at : col_at + cols_in]
    basis_in[...] = exact(inverses[0], factor_in)
    basis_out[...] = exact(inverses[1], factor_out)
    for value, start, size in ((basis_out, 0, cols_out), (basis_in, col_at, cols_in)):
        high, low = split(value[...])
        stack_ref[:, start : start + size] = jnp.concatenate([high, low, high], axis=0)
    for copy in pending:
        copy.wait_send()


def gram_roots(gram, turn, part, slots, copies, half):
    for copy in copies:
        copy.wait_recv()
    total = part[turn]
    for step in range(gram.count - 1):
        total = total + slots[turn, step]
    rank = 2 * half
    grams = []
    for place in (0, 2 * rank):
        grams.append(
            jnp.concatenate([total[:, place : place + rank], total[:, place + rank : place + 2 * rank]], axis=0)
        )
    return inverse_roots(grams)


def finish_kernel(
    offsets,
    steps,
    grads_in,
    error_in,
    weight_in,
    moment_in,
    grads_out,
    error_out,
    weight_out,
    moment_out,
    ortho_ref,
    stack_ref,
    master_in,
    velocity_in,
    residue_in,
    master_out,
    velocity_out,
    residue_out,
):
    row_at, col_at = offsets
    step = pl.program_id(0)
    for grads, error, weight, moment, master, velocity, residue, row, col in (
        (grads_in, error_in, weight_in, moment_in, master_in, velocity_in, residue_in, row_at, col_at),
        (grads_out, error_out, weight_out, moment_out, master_out, velocity_out, residue_out, 0, 0),
    ):
        rows, cols = weight.shape
        left = ortho_ref[pl.ds(pl.multiple_of(row + step * rows, 16), rows), :]
        approx = dot(left, stack_ref[:, col : col + cols], (1, 0))
        residue[0] = grads[0].astype(F32) + error[0] - approx
        speed = MOMENTUM_DECAY * moment[...] + approx
        velocity[...] = speed
        master[...] = weight[...] - LEARN_RATE * speed


def per_device(sizes, *arrays):
    grads_in, error_in, weight_in, moment_in, query_in = arrays[:5]
    grads_out, error_out, weight_out, moment_out, query_out = arrays[5:]
    replicas, shards, tensors = sizes
    rows_in, cols_in = weight_in.shape
    rows_out, cols_out = weight_out.shape
    rank = query_in.shape[1]
    row_at, col_at = up(rows_out, LANES), up(cols_out, LANES)
    left = Group(("replica", "tensor"), (replicas, tensors), rank, row_at + rows_in)
    right = Group(("replica", "shard"), (replicas, shards), rank, col_at + cols_in)
    gram = Group(("shard",), (shards,), rank, LANES)
    vmem = pl.BlockSpec(memory_space=pltpu.VMEM)
    packed = up(4 * rank, LANES)

    def room(group):
        return [
            pltpu.VMEM((ROUNDS, rank, group.total), F32),
            pltpu.VMEM((ROUNDS, group.slots(), group.rows, group.width), F32),
            pltpu.VMEM((ROUNDS, rank, group.total), F32),
        ]

    ortho, stack, basis_in, basis_out = pl.pallas_call(
        functools.partial(factors_kernel, left, right, gram, replicas),
        out_shape=(
            jax.ShapeDtypeStruct((row_at + up(rows_in, LANES), 3 * rank), BF16),
            jax.ShapeDtypeStruct((3 * rank, col_at + up(cols_in, LANES)), BF16),
            jax.ShapeDtypeStruct((rank, cols_in), F32),
            jax.ShapeDtypeStruct((rank, cols_out), F32),
        ),
        in_specs=[vmem] * 6,
        out_specs=(vmem,) * 4,
        scratch_shapes=[
            pltpu.VMEM((rows_in, cols_in), BF16),
            pltpu.VMEM((rows_in, cols_in), BF16),
            pltpu.VMEM((rows_out, cols_out), BF16),
            pltpu.VMEM((rows_out, cols_out), BF16),
            *room(left),
            *room(right),
            pltpu.VMEM((ROUNDS, rank // 2, packed), F32),
            pltpu.VMEM((ROUNDS, gram.slots(), rank // 2, packed), F32),
            pltpu.SemaphoreType.DMA((ROUNDS, 4, left.slots())),
            pltpu.SemaphoreType.DMA((ROUNDS, 4, right.slots())),
            pltpu.SemaphoreType.DMA((ROUNDS, 2, gram.slots())),
        ],
        compiler_params=pltpu.CompilerParams(collective_id=0, has_side_effects=True, vmem_limit_bytes=24 << 20),
        name="factors",
    )(grads_in, error_in, query_in.T, grads_out, error_out, query_out.T)

    steps = math.gcd(rows_in // 16, rows_out // 16, 4)

    def block(array):
        if array.ndim == 3:
            return pl.BlockSpec((1, array.shape[1] // steps, array.shape[2]), lambda step: (0, step, 0))
        return pl.BlockSpec((array.shape[0] // steps, array.shape[1]), lambda step: (step, 0))

    operands = (grads_in, error_in, weight_in, moment_in, grads_out, error_out, weight_out, moment_out)
    results = (weight_in, moment_in, error_in, weight_out, moment_out, error_out)
    finished = pl.pallas_call(
        functools.partial(finish_kernel, (row_at, col_at), steps),
        grid=(steps,),
        out_shape=tuple(jax.ShapeDtypeStruct(array.shape, F32) for array in results),
        in_specs=[block(array) for array in operands] + [vmem, vmem],
        out_specs=tuple(block(array) for array in results),
        compiler_params=pltpu.CompilerParams(vmem_limit_bytes=24 << 20),
        name="finish",
    )(*operands, ortho, stack)
    return (*finished[:3], basis_in.T, *finished[3:], basis_out.T)


def solution(mesh):
    sizes = (mesh.shape["replica"], mesh.shape["shard"], mesh.shape["tensor"])
    cube, flat, thin = P("replica", "shard", "tensor"), P("shard", "tensor"), P("tensor", None)
    return jax.shard_map(
        functools.partial(per_device, sizes),
        mesh=mesh,
        in_specs=(cube, cube, flat, flat, thin) * 2,
        out_specs=(flat, flat, cube, thin) * 2,
        check_vma=False,
    )
```

time: 378 us -> 56.8 us (0.15)
  blocking collectives: 169 us -> 0 us
  waiting for transfers between devices: 160 us -> 0 us
  Pallas kernels: 0 us -> 46.4 us
  matrix products: 27.3 us -> 0 us
  between operations: 17.1 us -> 0.69 us
  local copies, waits for them, and re-layouts: 1.32 us -> 9.19 us
    psum x6 -> x0, blocking collectives: 169 us -> none  [the longest x3 111 us: per_device(): lax.psum((precise_dot(projected_in.T, projected_in), precise_dot(projecte...]
    psum x3 -> x0, waiting for transfers between devices: 160 us -> none  [the longest x2 132 us: per_device(): lax.psum((column_in, column_out), ('replica', 'shard'))]
    pallas_call x0 -> x2, Pallas kernels: none -> 46.4 us  [the longest x1 43.9 us: per_device(): pl.pallas_call(functools.partial(factors_kernel, left, right, gram, repli...]
    dot_general x62 -> x0, matrix products: 27.3 us -> none  [the longest x58 22.1 us: precise_dot(): jnp.dot(left, right, precision=lax.Precision.HIGHEST, preferred_element_t...]
    unnamed x23 -> x24, local copies, waits for them, and re-layouts: 1.32 us -> 9.19 us
  transfers between devices with their start and end apart: 3 -> 0, of which waited for: 3 -> 0; matrix products, arithmetic and copies ran while one was open for 1% -> 0% of each run, Pallas kernels for 0% -> 0%
where the time goes in v1:
time: 56.8 us; the launch traced here: 56.3 us
  Pallas kernels  46.4 us (82%)
  local copies, waits for them, and re-layouts  9.19 us (16%)
  between operations  0.69 us (1%)
    pallas_call x1, Pallas kernels, per_device(): pl.pallas_call(functools.partial(factors_kernel, left, right, gram, repli...  43.9 us
    unnamed x24, local copies, waits for them, and re-layouts  9.19 us
    pallas_call x1, Pallas kernels, per_device(): pl.pallas_call(functools.partial(finish_kernel, (row_at, col_at), steps),...  2.54 us

profile of v1, /device:TPU:0, one launch (start us, length us, event | category | flops | bytes accessed | tf_op | source)
XLA Modules:
  0.0 56.3 jit_solution(8955848838605311278)
XLA Ops:
  0.6 0.0 copy-start
  0.6 1.1 %copy-done = f32[1,192,832]{2,1,0:T(8,128)S(1)} copy-done((f32[1,192,832]{2,1,0:T(8,128)S(1)}, f32[1,192,832]{2,1,0:T(8,128)}, u32[]{:S(2)}) %copy-start) | copy-done | bytes 639000
  1.7 0.0 copy-start.1
  1.7 1.1 %copy-done.1 = f32[1,384,384]{2,1,0:T(8,128)S(1)} copy-done((f32[1,384,384]{2,1,0:T(8,128)S(1)}, f32[1,384,384]{2,1,0:T(8,128)}, u32[]{:S(2)}) %copy-start.1) | copy-done | bytes 589848
  2.8 0.0 copy-start.3
  2.8 1.0 %copy-done.3 = bf16[1,192,832]{2,1,0:T(8,128)(2,1)S(1)} copy-done((bf16[1,192,832]{2,1,0:T(8,128)(2,1)S(1)}, bf16[1,192,832]{2,1,0:T(8,128)(2,1)}, u32[]{:S(2)}) %copy-start.3) | copy-done | bytes 319512
  3.8 0.0 copy-start.4
  3.8 1.0 %copy-done.4 = bf16[1,384,384]{2,1,0:T(8,128)(2,1)S(1)} copy-done((bf16[1,384,384]{2,1,0:T(8,128)(2,1)S(1)}, bf16[1,384,384]{2,1,0:T(8,128)(2,1)}, u32[]{:S(2)}) %copy-start.4) | copy-done | bytes 294936
  4.7 0.0 copy-start.9
  4.7 0.9 %copy-done.9 = f32[832,32]{0,1:T(8,128)S(1)} copy-done((f32[832,32]{0,1:T(8,128)S(1)}, f32[832,32]{0,1:T(8,128)}, u32[]{:S(2)}) %copy-start.9) | copy-done | bytes 106520
  5.6 0.0 copy-start.10
  5.6 0.8 %copy-done.10 = f32[384,32]{0,1:T(8,128)S(1)} copy-done((f32[384,32]{0,1:T(8,128)S(1)}, f32[384,32]{0,1:T(8,128)}, u32[]{:S(2)}) %copy-start.10) | copy-done | bytes 49176
  6.4 0.0 copy-start.2
  6.4 0.0 copy-start.5
  6.4 43.9 %factors.1 = (bf16[640,96]{1,0:T(8,128)(2,1)S(1)}, bf16[96,1280]{1,0:T(8,128)(2,1)S(1)}, f32[32,832]{1,0:T(8,128)S(1)}, f32[32,384]{1,0:T(8,128)S(1)}) custom-call(bf16[1,192,832]{2,1,0:T(8,128)(2,1)S(1)} %copy-done.3, f32[1,192,832]{2,1,0:T(8,128)S(1)} %copy-done, f32[32,832]{1,0:T(8,128)S(1)} %bitcast.5, bf16[1,384,384]{2,1,0:T(8,128)(2,1)S(1)} %copy-done.4, ...), custom_call_target="tpu_custom_call" | custom-call | tf_op jit(solution)/shard_map/factors/pallas_call | solution.py:323
  50.3 0.0 copy-done.2
  50.3 0.0 copy-done.5
  50.4 0.0 copy-done.6
  50.4 0.0 copy-start.7
  50.4 1.1 %copy-done.7 = f32[384,384]{1,0:T(8,128)S(1)} copy-done((f32[384,384]{1,0:T(8,128)S(1)}, f32[384,384]{1,0:T(8,128)}, u32[]{:S(2)}) %copy-start.7) | copy-done | bytes 589848
  51.4 1.1 %copy-done.8 = f32[384,384]{1,0:T(8,128)S(1)} copy-done((f32[384,384]{1,0:T(8,128)S(1)}, f32[384,384]{1,0:T(8,128)}, u32[]{:S(2)}) %copy-start.8) | copy-done | bytes 589848
  52.5 2.5 %finish.1 = (f32[192,832]{1,0:T(8,128)}, f32[192,832]{1,0:T(8,128)}, f32[1,192,832]{2,1,0:T(8,128)}, f32[384,384]{1,0:T(8,128)}, f32[384,384]{1,0:T(8,128)}, /*index=5*/f32[1,384,384]{2,1,0:T(8,128)}) custom-call(bf16[1,192,832]{2,1,0:T(8,128)(2,1)S(1)} %copy-done.3, f32[1,192,832]{2,1,0:T(8,128)S(1)} %copy-done, f32[192,832]{1,0:T(8,128)S(1)} %copy-done.5, ...), custom_call_target="tpu_custom_call" | custom-call | tf_op jit(solution)/shard_map/finish/pallas_call | solution.py:359
  55.0 0.6 %copy.20 = f32[832,32]{0,1:T(8,128)} copy(f32[832,32]{0,1:T(8,128)S(1)} %bitcast.4) | data formatting | bytes 212992
  55.7 0.6 %copy.21 = f32[384,32]{0,1:T(8,128)} copy(f32[384,32]{0,1:T(8,128)S(1)} %bitcast.6) | data formatting | bytes 98304
  (2 shorter events, 0.0 us)
Async XLA Ops:
  0.6 1.1 %copy-start = (f32[1,192,832]{2,1,0:T(8,128)S(1)}, f32[1,192,832]{2,1,0:T(8,128)}, u32[]{:S(2)}) copy-start(f32[1,192,832]{2,1,0:T(8,128)} %error_in.3) | copy-start | bytes 1916932
  1.7 1.1 %copy-start.1 = (f32[1,384,384]{2,1,0:T(8,128)S(1)}, f32[1,384,384]{2,1,0:T(8,128)}, u32[]{:S(2)}) copy-start(f32[1,384,384]{2,1,0:T(8,128)} %error_out.3) | copy-start | bytes 1769476
  2.8 1.0 %copy-start.3 = (bf16[1,192,832]{2,1,0:T(8,128)(2,1)S(1)}, bf16[1,192,832]{2,1,0:T(8,128)(2,1)}, u32[]{:S(2)}) copy-start(bf16[1,192,832]{2,1,0:T(8,128)(2,1)} %grads_in.3) | copy-start | bytes 958468
  3.8 1.0 %copy-start.4 = (bf16[1,384,384]{2,1,0:T(8,128)(2,1)S(1)}, bf16[1,384,384]{2,1,0:T(8,128)(2,1)}, u32[]{:S(2)}) copy-start(bf16[1,384,384]{2,1,0:T(8,128)(2,1)} %grads_out.3) | copy-start | bytes 884740
  4.7 0.9 %copy-start.9 = (f32[832,32]{0,1:T(8,128)S(1)}, f32[832,32]{0,1:T(8,128)}, u32[]{:S(2)}) copy-start(f32[832,32]{0,1:T(8,128)} %param.14) | copy-start | bytes 319492
  5.6 0.8 %copy-start.10 = (f32[384,32]{0,1:T(8,128)S(1)}, f32[384,32]{0,1:T(8,128)}, u32[]{:S(2)}) copy-start(f32[384,32]{0,1:T(8,128)} %param.19) | copy-start | bytes 147460
  6.4 43.9 %copy-start.2 = (f32[1,384,384]{2,1,0:T(8,128)S(1)}, f32[1,384,384]{2,1,0:T(8,128)}, u32[]{:S(2)}) copy-start(f32[1,384,384]{2,1,0:T(8,128)} %error_out.3) | copy-start | bytes 1769476
  6.4 43.9 %copy-start.5 = (f32[192,832]{1,0:T(8,128)S(1)}, f32[192,832]{1,0:T(8,128)}, u32[]{:S(2)}) copy-start(f32[192,832]{1,0:T(8,128)} %weight_in.1) | copy-start | bytes 1916932
  6.4 43.9 %copy-start.6 = (f32[192,832]{1,0:T(8,128)S(1)}, f32[192,832]{1,0:T(8,128)}, u32[]{:S(2)}) copy-start(f32[192,832]{1,0:T(8,128)} %moment_in.1) | copy-start | bytes 1916932
  50.4 1.1 %copy-start.7 = (f32[384,384]{1,0:T(8,128)S(1)}, f32[384,384]{1,0:T(8,128)}, u32[]{:S(2)}) copy-start(f32[384,384]{1,0:T(8,128)} %weight_out.1) | copy-start | bytes 1769476
  51.4 1.1 %copy-start.8 = (f32[384,384]{1,0:T(8,128)S(1)}, f32[384,384]{1,0:T(8,128)}, u32[]{:S(2)}) copy-start(f32[384,384]{1,0:T(8,128)} %moment_out.1) | copy-start | bytes 1769476

commit v2 on v1

v2 whole, which is shorter than its diff:
```python
import functools
import math

import jax
import jax.numpy as jnp
from jax import lax
from jax.experimental import pallas as pl
from jax.experimental.pallas import tpu as pltpu
from jax.sharding import PartitionSpec as P

ROUNDS = 2
NS_STEPS = 4
MOMENTUM_DECAY = 0.9
LEARN_RATE = 0.1
EPSILON = 1e-06
LANES = 128
MESH = pl.DeviceIdType.MESH
F32 = jnp.float32
BF16 = jnp.bfloat16


def up(value, multiple):
    return -(-value // multiple) * multiple


def split(value):
    high = value.astype(BF16)
    low = (value - high.astype(F32)).astype(BF16)
    return high, low


def dot(left, right, contract):
    return lax.dot_general(left, right, ((contract[:1], contract[1:]), ((), ())), preferred_element_type=F32)


def exact(left, right, contract=(1, 0)):
    return lax.dot_general(
        left,
        right,
        ((contract[:1], contract[1:]), ((), ())),
        precision=lax.Precision.HIGHEST,
        preferred_element_type=F32,
    )


def by_matrix(factor, high_ref, low_ref, contract):
    rank = factor.shape[0]
    high, low = split(factor)
    both = dot(jnp.concatenate([high, low], axis=0), high_ref[...], contract)
    return both[:rank] + both[rank:] + dot(high, low_ref[...], contract)


def inverse_roots(grams):
    rank = grams[0].shape[0]
    identity = (
        lax.broadcasted_iota(jnp.int32, (rank, rank), 0) == lax.broadcasted_iota(jnp.int32, (rank, rank), 1)
    ).astype(F32)
    scales = [jnp.sqrt(jnp.sum(gram * gram, keepdims=True) + EPSILON) for gram in grams]
    currents = [gram / scale for gram, scale in zip(grams, scales)]
    inverses = [identity for gram in grams]
    for sweep in range(NS_STEPS):
        products = [current if sweep == 0 else exact(inverse, current) for inverse, current in zip(inverses, currents)]
        middles = [0.5 * (3.0 * identity - product) for product in products]
        inverses = [middle if sweep == 0 else exact(middle, inverse) for middle, inverse in zip(middles, inverses)]
        if sweep < NS_STEPS - 1:
            currents = [exact(current, middle) for current, middle in zip(currents, middles)]
    return [inverse / jnp.sqrt(scale) for inverse, scale in zip(inverses, scales)]


class Group:
    def __init__(self, axes, sizes, rank, width):
        self.axes = axes
        self.sizes = sizes
        self.count = math.prod(sizes)
        self.down = math.gcd(self.count, max(rank // 8, 1))
        self.across = self.count // self.down
        self.rows = rank // self.down
        self.total = up(width, LANES * self.across)
        self.width = self.total // self.across

    def index(self):
        index = 0
        for axis, size in zip(self.axes, self.sizes):
            index = index * size + lax.axis_index(axis)
        return index

    def place(self):
        index = self.index()
        return lax.div(index, self.across), lax.rem(index, self.across)

    def device(self, down, across):
        index = down * self.across + across
        place = {name: lax.axis_index(name) for name in ("replica", "shard", "tensor")}
        for axis, size in reversed(list(zip(self.axes, self.sizes))):
            place[axis] = lax.rem(index, size)
            index = lax.div(index, size)
        return (place["replica"], place["shard"], place["tensor"])

    def near(self):
        down, across = self.place()
        return [
            ((self.down - 1) * self.across + step - 1, down, lax.rem(across + step, self.across))
            for step in range(1, self.across)
        ]

    def far(self, across):
        down, mine = self.place()
        return [
            ((step - 1) * self.across + mine, lax.rem(down + step, self.down), across) for step in range(1, self.down)
        ]

    def peers(self):
        return [peer for part in range(self.across) for peer in self.far(part)] + self.near()

    def near_slots(self):
        return [(self.down - 1) * self.across + step - 1 for step in range(1, self.across)]

    def far_slots(self, across):
        return [(step - 1) * self.across + across for step in range(1, self.down)]

    def all_slots(self):
        return range(self.count - 1)

    def piece(self, down, across):
        row = pl.multiple_of(down * self.rows, 8)
        lane = 0 if self.across == 1 else pl.multiple_of(across * self.width, LANES)
        return (pl.ds(row, self.rows), pl.ds(lane, self.width))

    def slots(self):
        return max(self.count - 1, 1)


class Exchange:
    def __init__(self, group, replicas, part, slots, total, sems):
        self.group, self.replicas = group, replicas
        self.part, self.slots, self.total, self.sems = part, slots, total, sems
        self.started = []

    def copy(self, source, target, stage, slot, peer):
        return pltpu.make_async_remote_copy(
            src_ref=source,
            dst_ref=target,
            send_sem=self.sems.at[stage, slot],
            recv_sem=self.sems.at[stage + 1, slot],
            device_id=self.group.device(*peer),
            device_id_type=MESH,
        )

    def start(self, copy):
        copy.start()
        self.started.append(copy)

    def scatter(self, peers):
        for slot, *peer in peers:
            self.start(self.copy(self.part.at[self.group.piece(*peer)], self.slots.at[slot], 0, slot, peer))

    def arrive(self, stage, slots, target):
        place = self.group.place()
        for slot in slots:
            target_ref = target(slot)
            self.copy(target_ref, target_ref, stage, slot, place).wait_recv()

    def gather(self):
        group = self.group
        self.arrive(0, group.all_slots(), lambda slot: self.slots.at[slot])
        piece = group.piece(*group.place())
        mine = self.part.at[piece][...]
        for slot in group.all_slots():
            mine = mine + self.slots[slot]
        if self.replicas > 1:
            mine = mine * (1.0 / self.replicas)
        own = self.total.at[piece]
        own[...] = mine
        for slot, *peer in group.peers():
            self.start(self.copy(own, own, 2, slot, peer))

    def finish(self, slots):
        own = self.total.at[self.group.piece(*self.group.place())]
        self.arrive(2, slots, lambda slot: own)

    def broadcast(self):
        for slot, *peer in self.group.peers():
            self.start(self.copy(self.part, self.slots.at[slot], 0, slot, peer))

    def collect(self):
        self.arrive(0, self.group.all_slots(), lambda slot: self.slots.at[slot])
        total = self.part[...]
        for slot in self.group.all_slots():
            total = total + self.slots[slot]
        return total


def factors_kernel(groups, replicas, *refs):
    left_out, left_in, right, gram = groups
    sources, refs = refs[:10], refs[10:]
    merged, weights, moments, refs = refs[:2], refs[2:4], refs[4:6], refs[6:]
    ortho_ref, stack_ref, bases, refs = refs[0], refs[1], refs[2:4], refs[4:]
    grads, errors, queries, refs = refs[:2], refs[2:4], refs[4:6], refs[6:]
    highs, lows, refs = refs[:2], refs[2:4], refs[4:]
    load_sems, rooms = refs[0], [refs[1 + 4 * place : 5 + 4 * place] for place in range(4)]
    rank = queries[0].shape[0]
    half = rank // 2
    (rows_in, cols_in), (rows_out, cols_out) = merged[0].shape, merged[1].shape
    row_at, col_at = up(rows_out, LANES), up(cols_out, LANES)
    gram_at = col_at + cols_in
    targets = (
        grads[0], errors[0], weights[0], moments[0], queries[0],
        grads[1], errors[1], weights[1], moments[1], queries[1],
    )
    loads = [
        pltpu.make_async_copy(source, target, load_sems.at[place])
        for place, (source, target) in enumerate(zip(sources, targets))
    ]
    for place in (6, 5, 9, 1, 0, 4, 2, 3, 7, 8):
        loads[place].start()

    barrier = pltpu.get_barrier_semaphore()
    greeted = 0
    for group in groups:
        for slot, *peer in group.peers():
            pl.semaphore_signal(barrier, inc=1, device_id=group.device(*peer), device_id_type=MESH)
            greeted += 1

    for part in (rooms[0][0], rooms[1][0], rooms[2][0]):
        part[...] = jnp.zeros_like(part)
    exchanges = [
        [
            Exchange(group, count, part.at[turn], slots.at[turn], total.at[turn], sems.at[turn])
            for group, count, (part, slots, total, sems) in zip(groups, (replicas, replicas, replicas, 1), rooms)
        ]
        for turn in range(ROUNDS)
    ]

    def merge(which, first):
        for place in (first, first + 1, first + 4):
            loads[place].wait()
        value = grads[which][0].astype(F32) + errors[which][0]
        merged[which][...] = value
        highs[which][...], lows[which][...] = split(value)

    inverses = None
    for turn in range(ROUNDS):
        sum_out, sum_in, sum_right, sum_gram = exchanges[turn]
        if turn == 0:
            merge(1, 5)
            factor_out = queries[1][...]
        else:
            before = exchanges[turn - 1][2]
            before.finish(right.near_slots())
            waited = 0
            while waited * right.width < cols_out:
                before.finish(right.far_slots(waited))
                waited += 1
            factor_out = before.total[:, :cols_out]
        sum_out.part[:, :rows_out] = by_matrix(factor_out, highs[1], lows[1], (1, 1))
        if turn == 0:
            pl.semaphore_wait(barrier, greeted)
        sum_out.scatter(sum_out.group.peers())
        if turn == 0:
            merge(0, 0)
            factor_in = queries[0][...]
        else:
            for part in range(waited, right.across):
                before.finish(right.far_slots(part))
            factor_in = before.total[:, col_at : col_at + cols_in]
        sum_in.part[:, :rows_in] = by_matrix(factor_in, highs[0], lows[0], (1, 1))
        sum_in.scatter(sum_in.group.peers())
        sum_out.gather()
        sum_in.gather()
        if turn > 0:
            grams = before.total[:, gram_at : gram_at + 2 * rank]
            inverses = inverse_roots((grams[:, :rank], grams[:, rank:]))
        sum_out.finish(left_out.all_slots())
        projected_out = sum_out.total[:, :rows_out]
        if turn > 0:
            projected_out = exact(inverses[1], projected_out)
        sum_right.part[:, :cols_out] = by_matrix(projected_out, highs[1], lows[1], (1, 0))
        sum_in.finish(left_in.all_slots())
        projected_in = sum_in.total[:, :rows_in]
        if turn > 0:
            projected_in = exact(inverses[0], projected_in)
        products = [exact(value, value, (1, 1)) for value in (projected_in, projected_out)]
        if turn < ROUNDS - 1:
            for place, product in enumerate(products):
                start = gram_at + place * rank
                sum_right.part[:, start : start + rank] = product
        else:
            for place, product in enumerate(products):
                for step in range(2):
                    start = (2 * place + step) * rank
                    sum_gram.part[:, start : start + rank] = product[step * half : step * half + half]
            sum_gram.broadcast()
        done = col_at
        for part in range(right.across):
            stop = min((part + 1) * right.width, gram_at)
            if stop > done:
                columns = (slice(None), slice(done - col_at, stop - col_at))
                sum_right.part[:, done:stop] = by_matrix(projected_in, highs[0].at[columns], lows[0].at[columns], (1, 0))
                done = stop
            sum_right.scatter(right.far(part))
        sum_right.scatter(right.near())
        sum_right.gather()
    for place in (2, 3, 7, 8):
        loads[place].wait()
    total = sum_gram.collect()
    grams = [
        jnp.concatenate([total[:, place : place + rank], total[:, place + rank : place + 2 * rank]], axis=0)
        for place in (0, 2 * rank)
    ]
    inverses = inverse_roots(grams)
    for value, inverse, start, size in (
        (projected_out, inverses[1], 0, rows_out),
        (projected_in, inverses[0], row_at, rows_in),
    ):
        high, low = split(exact(inverse, value))
        tall = jnp.concatenate([high, high, low], axis=0).astype(F32)
        ortho_ref[start : start + size, :] = jnp.transpose(tall).astype(BF16)
    sum_right.finish(right.all_slots())
    for which, start, size in ((1, 0, cols_out), (0, col_at, cols_in)):
        value = exact(inverses[which], sum_right.total[:, start : start + size])
        bases[which][...] = value
        high, low = split(value)
        stack_ref[:, start : start + size] = jnp.concatenate([high, low, high], axis=0)
    for turn in exchanges:
        for exchange in turn:
            for copy in exchange.started:
                copy.wait_send()


def finish_kernel(offsets, *refs):
    merged, weights, moments, refs = refs[:2], refs[2:4], refs[4:6], refs[6:]
    ortho_ref, stack_ref, bases, refs = refs[0], refs[1], refs[2:4], refs[4:]
    outputs = (refs[:4], refs[4:])
    step = pl.program_id(0)

    @pl.when(step == 0)
    def _():
        for basis, output in zip(bases, outputs):
            output[3][...] = basis[...]

    for which, (row, col) in enumerate((offsets, (0, 0))):
        master, velocity, residue = outputs[which][:3]
        rows, cols = master.shape
        here = pl.ds(pl.multiple_of(step * rows, 16), rows)
        left = ortho_ref[pl.ds(pl.multiple_of(row + step * rows, 16), rows), :]
        approx = dot(left, stack_ref[:, col : col + cols], (1, 0))
        residue[0] = merged[which][here, :] - approx
        speed = MOMENTUM_DECAY * moments[which][here, :] + approx
        velocity[...] = speed
        master[...] = weights[which][here, :] - LEARN_RATE * speed


def per_device(sizes, *arrays):
    weight_in, weight_out, query_in = arrays[2], arrays[7], arrays[4]
    replicas, shards, tensors = sizes
    rows_in, cols_in = weight_in.shape
    rows_out, cols_out = weight_out.shape
    rank = query_in.shape[1]
    row_at, col_at = up(rows_out, LANES), up(cols_out, LANES)
    left_axes = (("replica", "tensor"), (replicas, tensors), rank)
    left_out, left_in = Group(*left_axes, rows_out), Group(*left_axes, rows_in)
    right = Group(("replica", "shard"), (replicas, shards), rank, col_at + cols_in + 2 * rank)
    gram = Group(("shard",), (shards,), rank, LANES)
    groups = (left_out, left_in, right, gram)
    vmem = pl.BlockSpec(memory_space=pltpu.VMEM)
    packed = up(4 * rank, LANES)

    def room(group):
        return [
            pltpu.VMEM((ROUNDS, rank, group.total), F32),
            pltpu.VMEM((ROUNDS, group.slots(), group.rows, group.width), F32),
            pltpu.VMEM((ROUNDS, rank, group.total), F32),
            pltpu.SemaphoreType.DMA((ROUNDS, 4, group.slots())),
        ]

    both = (weight_in.shape, weight_out.shape)
    operands = [array.T if array.shape[-1] == rank else array for array in arrays]
    operands = [pltpu.with_memory_space_constraint(array, pltpu.HBM) for array in operands]
    carried = pl.pallas_call(
        functools.partial(factors_kernel, groups, replicas),
        out_shape=(
            *[jax.ShapeDtypeStruct(shape, F32) for shape in both * 3],
            jax.ShapeDtypeStruct((row_at + up(rows_in, LANES), 3 * rank), BF16),
            jax.ShapeDtypeStruct((3 * rank, col_at + up(cols_in, LANES)), BF16),
            jax.ShapeDtypeStruct((rank, cols_in), F32),
            jax.ShapeDtypeStruct((rank, cols_out), F32),
        ),
        in_specs=[pl.BlockSpec(memory_space=pltpu.HBM)] * 10,
        out_specs=(vmem,) * 10,
        scratch_shapes=[
            *[pltpu.VMEM((1, *shape), BF16) for shape in both],
            *[pltpu.VMEM((1, *shape), F32) for shape in both],
            *[pltpu.VMEM((rank, shape[1]), F32) for shape in both],
            *[pltpu.VMEM(shape, BF16) for shape in both * 2],
            pltpu.SemaphoreType.DMA((10,)),
            *[space for group in groups[:3] for space in room(group)],
            pltpu.VMEM((ROUNDS, rank // 2, packed), F32),
            pltpu.VMEM((ROUNDS, gram.slots(), rank // 2, packed), F32),
            pltpu.VMEM((ROUNDS, 8, packed), F32),
            pltpu.SemaphoreType.DMA((ROUNDS, 2, gram.slots())),
        ],
        compiler_params=pltpu.CompilerParams(collective_id=0, has_side_effects=True, vmem_limit_bytes=24 << 20),
        name="factors",
    )(*operands)

    steps = math.gcd(rows_in // 16, rows_out // 16, 4)

    def rows_of(shape):
        return pl.BlockSpec((shape[0] // steps, shape[1]), lambda step: (step, 0))

    def cube_of(shape):
        return pl.BlockSpec((1, shape[0] // steps, shape[1]), lambda step: (0, step, 0))

    results, specs = [], []
    for shape in both:
        results += [shape, shape, (1, *shape), (rank, shape[1])]
        specs += [rows_of(shape), rows_of(shape), cube_of(shape), pl.BlockSpec((rank, shape[1]), lambda step: (0, 0))]
    finished = pl.pallas_call(
        functools.partial(finish_kernel, (row_at, col_at)),
        grid=(steps,),
        out_shape=tuple(jax.ShapeDtypeStruct(shape, F32) for shape in results),
        in_specs=[vmem] * 10,
        out_specs=tuple(specs),
        compiler_params=pltpu.CompilerParams(vmem_limit_bytes=24 << 20),
        name="finish",
    )(*carried)
    return tuple(array.T if place % 4 == 3 else array for place, array in enumerate(finished))


def solution(mesh):
    sizes = (mesh.shape["replica"], mesh.shape["shard"], mesh.shape["tensor"])
    cube, flat, thin = P("replica", "shard", "tensor"), P("shard", "tensor"), P("tensor", None)
    return jax.shard_map(
        functools.partial(per_device, sizes),
        mesh=mesh,
        in_specs=(cube, cube, flat, flat, thin) * 2,
        out_specs=(flat, flat, cube, thin) * 2,
        check_vma=False,
    )
```

time: 56.8 us -> 45.8 us (0.81)
  local copies, waits for them, and re-layouts: 9.19 us -> 0 us
  Pallas kernels: 46.4 us -> 45 us
    unnamed x24 -> x0, local copies, waits for them, and re-layouts: 9.19 us -> none
    pallas_call x2, Pallas kernels: 46.4 us -> 45 us  [the longest x1 42.4 us: per_device(): pl.pallas_call(functools.partial(factors_kernel, groups, replicas), out_s...]
where the time goes in v2:
time: 45.8 us; the launch traced here: 45.7 us
  Pallas kernels  45 us (98%)
  between operations  0.64 us (1%)
    pallas_call x1, Pallas kernels, per_device(): pl.pallas_call(functools.partial(factors_kernel, groups, replicas), out_s...  42.4 us
    pallas_call x1, Pallas kernels, per_device(): pl.pallas_call(functools.partial(finish_kernel, (row_at, col_at)), grid=(...  2.65 us

profile of v2, /device:TPU:0, one launch (start us, length us, event | category | flops | bytes accessed | tf_op | source)
XLA Modules:
  0.0 45.7 jit_solution(15711203727834106101)
XLA Ops:
  0.6 42.4 %factors.1 = (f32[192,832]{1,0:T(8,128)S(1)}, f32[384,384]{1,0:T(8,128)S(1)}, f32[192,832]{1,0:T(8,128)S(1)}, f32[384,384]{1,0:T(8,128)S(1)}, f32[192,832]{1,0:T...) custom-call(bf16[1,192,832]{2,1,0:T(8,128)(2,1)} %refs_0_.1, ...), custom_call_target="tpu_custom_call" | custom-call | tf_op jit(solution)/shard_map/factors/pallas_call | solution.py:379
  43.0 2.7 %finish.1 = (f32[192,832]{1,0:T(8,128)}, f32[192,832]{1,0:T(8,128)}, f32[1,192,832]{2,1,0:T(8,128)}, f32[32,832]{1,0:T(8,128)}, f32[384,384]{1,0:T(8,128)}, /*in...) custom-call(f32[192,832]{1,0:T(8,128)S(1)} %get-tuple-element.26.refs_0_, ...), custom_call_target="tpu_custom_call" | custom-call | tf_op jit(solution)/shard_map/finish/pallas_call | solution.py:418

commit v3 on v2

--- a/solution.py
+++ b/solution.py
@@ -33,21 +33,19 @@
     return lax.dot_general(left, right, ((contract[:1], contract[1:]), ((), ())), preferred_element_type=F32)
 
 
-def exact(left, right, contract=(1, 0)):
-    return lax.dot_general(
-        left,
-        right,
-        ((contract[:1], contract[1:]), ((), ())),
-        precision=lax.Precision.HIGHEST,
-        preferred_element_type=F32,
-    )
-
-
-def by_matrix(factor, high_ref, low_ref, contract):
+def by_parts(factor, parts, contract):
     rank = factor.shape[0]
     high, low = split(factor)
-    both = dot(jnp.concatenate([high, low], axis=0), high_ref[...], contract)
-    return both[:rank] + both[rank:] + dot(high, low_ref[...], contract)
+    both = dot(jnp.concatenate([high, low], axis=0), parts[0], contract)
+    return both[:rank] + both[rank:] + dot(high, parts[1], contract)
+
+
+def by_matrix(factor, high_ref, low_ref, contract):
+    return by_parts(factor, (high_ref[...], low_ref[...]), contract)
+
+
+def product_of(left, right, contract=(1, 0)):
+    return by_parts(left, split(right), contract)
 
 
 def inverse_roots(grams):
@@ -59,11 +57,11 @@
     currents = [gram / scale for gram, scale in zip(grams, scales)]
     inverses = [identity for gram in grams]
     for sweep in range(NS_STEPS):
-        products = [current if sweep == 0 else exact(inverse, current) for inverse, current in zip(inverses, currents)]
+        products = [current if sweep == 0 else product_of(inverse, current) for inverse, current in zip(inverses, currents)]
         middles = [0.5 * (3.0 * identity - product) for product in products]
-        inverses = [middle if sweep == 0 else exact(middle, inverse) for middle, inverse in zip(middles, inverses)]
+        inverses = [middle if sweep == 0 else product_of(middle, inverse) for middle, inverse in zip(middles, inverses)]
         if sweep < NS_STEPS - 1:
-            currents = [exact(current, middle) for current, middle in zip(currents, middles)]
+            currents = [product_of(current, middle) for current, middle in zip(currents, middles)]
     return [inverse / jnp.sqrt(scale) for inverse, scale in zip(inverses, scales)]
 
 
@@ -273,13 +271,13 @@
         sum_out.finish(left_out.all_slots())
         projected_out = sum_out.total[:, :rows_out]
         if turn > 0:
-            projected_out = exact(inverses[1], projected_out)
+            projected_out = product_of(inverses[1], projected_out)
         sum_right.part[:, :cols_out] = by_matrix(projected_out, highs[1], lows[1], (1, 0))
         sum_in.finish(left_in.all_slots())
         projected_in = sum_in.total[:, :rows_in]
         if turn > 0:
-            projected_in = exact(inverses[0], projected_in)
-        products = [exact(value, value, (1, 1)) for value in (projected_in, projected_out)]
+            projected_in = product_of(inverses[0], projected_in)
+        products = [product_of(value, value, (1, 1)) for value in (projected_in, projected_out)]
         if turn < ROUNDS - 1:
             for place, product in enumerate(products):
                 start = gram_at + place * rank
@@ -312,12 +310,12 @@
         (projected_out, inverses[1], 0, rows_out),
         (projected_in, inverses[0], row_at, rows_in),
     ):
-        high, low = split(exact(inverse, value))
+        high, low = split(product_of(inverse, value))
         tall = jnp.concatenate([high, high, low], axis=0).astype(F32)
         ortho_ref[start : start + size, :] = jnp.transpose(tall).astype(BF16)
     sum_right.finish(right.all_slots())
     for which, start, size in ((1, 0, cols_out), (0, col_at, cols_in)):
-        value = exact(inverses[which], sum_right.total[:, start : start + size])
+        value = product_of(inverses[which], sum_right.total[:, start : start + size])
         bases[which][...] = value
         high, low = split(value)
         stack_ref[:, start : start + size] = jnp.concatenate([high, low, high], axis=0)

time: 45.8 us -> 45.6 us (level)
  no operation moved by 1% of the time
where the time goes in v3:
time: 45.6 us; the launch traced here: 45.4 us
  Pallas kernels  44.8 us (98%)
  between operations  0.64 us (1%)
    pallas_call x1, Pallas kernels, per_device(): pl.pallas_call(functools.partial(factors_kernel, groups, replicas), out_s...  42.1 us
    pallas_call x1, Pallas kernels, per_device(): pl.pallas_call(functools.partial(finish_kernel, (row_at, col_at)), grid=(...  2.65 us

profile of v3, /device:TPU:0, one launch (start us, length us, event | category | flops | bytes accessed | tf_op | source)
XLA Modules:
  0.0 45.4 jit_solution(6883581031680434779)
XLA Ops:
  0.6 42.1 %factors.1 = (f32[192,832]{1,0:T(8,128)S(1)}, f32[384,384]{1,0:T(8,128)S(1)}, f32[192,832]{1,0:T(8,128)S(1)}, f32[384,384]{1,0:T(8,128)S(1)}, f32[192,832]{1,0:T...) custom-call(bf16[1,192,832]{2,1,0:T(8,128)(2,1)} %refs_0_.1, ...), custom_call_target="tpu_custom_call" | custom-call | tf_op jit(solution)/shard_map/factors/pallas_call | solution.py:377
  42.8 2.7 %finish.1 = (f32[192,832]{1,0:T(8,128)}, f32[192,832]{1,0:T(8,128)}, f32[1,192,832]{2,1,0:T(8,128)}, f32[32,832]{1,0:T(8,128)}, f32[384,384]{1,0:T(8,128)}, /*in...) custom-call(f32[192,832]{1,0:T(8,128)S(1)} %get-tuple-element.26.refs_0_, ...), custom_call_target="tpu_custom_call" | custom-call | tf_op jit(solution)/shard_map/finish/pallas_call | solution.py:416
